TPU v7x, 256 devices: a whole 4x4x8 slice. The times are simulated.
256 devices in a mesh: ctx: 32 (over x, z), head: 8 (over y, core).
Axes of the slice: x: 4, y: 4, z: 8, core: 2. Of those that a mesh axis runs over, the one named last changes fastest.
Arguments:
- ssm_input: bfloat16 [8192, 8192], P('ctx', 'head'), may hold values from -6 to 6
- gate_input: bfloat16 [8192, 8192], P('ctx', 'head'), may hold values from -6 to 6
- in_state: bfloat16 [8192, 1024], P('ctx', 'head'), may hold values from -0.5 to 0.5
- out_state: bfloat16 [8192, 1024], P('ctx', 'head'), may hold values from -0.5 to 0.5
- step_size: float32 [8192, 128], P('ctx', 'head'), may hold values from 0.05 to 0.5
- log_decay: float32 [8192, 128], P('ctx', 'head'), may hold values from 0 to 2
- skip_gain: float32 [128], P('head'), may hold values from 0.5 to 1.5
- norm_gain: float32 [8192], P('head'), may hold values from 0.5 to 1.5
- queries: bfloat16 [8192, 8192], P('ctx', 'head'), may hold values from -5 to 5
- keys: bfloat16 [8192, 1024], P('ctx', 'head'), may hold values from -5 to 5
- values: bfloat16 [8192, 1024], P('ctx', 'head'), may hold values from -6 to 6
Outputs:
- mamba_out: bfloat16 [8192, 8192], P('ctx', 'head')
- attention_out: bfloat16 [8192, 8192], P('ctx', 'head')
All inputs are finite; a program needn't handle non-finite values.
Results may differ from a plain program's by a relative error of at most 0.014.
Values may be sent and summed in bfloat16 or wider, within the bound.
No kernel may reach another device: no remote copies, remote signals or barrier semaphores. Data moves between devices by JAX's collectives and lax.ppermute only.
A program may use at most 128 MiB of HBM per device.

v0:
```python
import jax
import jax.numpy as jnp
from jax import lax
from jax.sharding import PartitionSpec as P

MIXER_HEADS = 128
P_SIZE = 64
N = 128
HQ = 64
KVH = 8
DH = 128
BLOCK = 256
HIGH = lax.Precision.HIGHEST


def carried_in(value, axis, join, neutral):
    place = lax.axis_index(axis)
    gathered = jax.tree.map(
        lambda a, kind: lax.all_gather(a.astype(kind), axis), value, (jnp.bfloat16, jnp.bfloat16)
    )
    state = jax.tree.map(lambda a, e: jnp.zeros_like(a) + jnp.asarray(e, a.dtype), value, neutral)

    def one(turn, state):
        return join(
            state,
            jax.tree.map(
                lambda a, own: lax.dynamic_index_in_dim(a, turn, 0, False).astype(own.dtype),
                gathered,
                value,
            ),
        )

    return lax.fori_loop(0, place, one, state)


def block_segments(signal, enter, enter_half, leave_half, step_size, decay):
    length = signal.shape[0]
    running_state = jnp.cumsum(decay, axis=0)
    scaled = signal * step_size[..., None]
    affinity = jnp.einsum(
        "tgn,sgn->tsg", leave_half, enter_half, preferred_element_type=jnp.float32
    )
    order = jnp.arange(length, dtype=jnp.int32)
    causal = (order[:, None] >= order[None, :])[:, :, None, None]
    spread = jnp.where(causal, running_state[:, None] - running_state[None, :], 0.0)
    mixing = jnp.where(causal, jnp.exp(-spread), 0.0) * affinity[..., None]
    within_block = jnp.einsum("tsgk,sgkp->tgkp", mixing, scaled, precision=HIGH)
    total_sum = running_state[-1]
    remain = jnp.exp(running_state - total_sum[None])
    state_contribution = jnp.einsum(
        "sgn,sgkp->gknp", enter, scaled * remain[..., None], precision=HIGH
    )
    return (within_block, state_contribution, jnp.exp(-total_sum), running_state, total_sum)


def past_carryover(leave, running_state, state_matrix):
    return (
        jnp.einsum("tgn,gknp->tgkp", leave, state_matrix, precision=HIGH)
        * jnp.exp(-running_state)[..., None]
    )


def mamba_mixer(
    ssm_input, gate_input, in_state, out_state, step_size, log_decay, skip_gain, norm_gain
):
    tokens_here = ssm_input.shape[0]
    count = tokens_here // BLOCK
    heads_here = skip_gain.shape[0]
    groups_here = in_state.shape[1] // N
    per_group = heads_here // groups_here
    signal = ssm_input.astype(jnp.float32).reshape(count, BLOCK, groups_here, per_group, P_SIZE)
    enter_half = in_state.reshape(count, BLOCK, groups_here, N)
    leave_half = out_state.reshape(count, BLOCK, groups_here, N)
    enter = enter_half.astype(jnp.float32)
    leave = leave_half.astype(jnp.float32)
    stepped = step_size.reshape(count, BLOCK, groups_here, per_group)
    decay = log_decay.reshape(count, BLOCK, groups_here, per_group)
    skip_path = skip_gain.reshape(groups_here, per_group)
    pieces = block_segments(signal[0], enter[0], enter_half[0], leave_half[0], stepped[0], decay[0])
    fade_all = jnp.ones((groups_here, per_group), jnp.float32)
    carried = jnp.zeros((groups_here, per_group, N, P_SIZE), jnp.float32)
    carried = pieces[2][..., None, None] * carried + pieces[1]
    fade_all = fade_all * pieces[2]

    def combine(earlier, later):
        return (earlier[0] * later[0], later[0][..., None, None] * earlier[1] + later[1])

    identity = (jnp.ones_like(fade_all), jnp.zeros_like(carried))
    _, state_matrix = carried_in((fade_all, carried), "ctx", combine, identity)
    within_block, state_contribution, fading_factor, running_state, total_sum = pieces
    mixed_output = (
        within_block
        + past_carryover(leave[0], running_state, state_matrix)
        + skip_path[..., None] * signal[0]
    )
    outputs = [mixed_output]
    mixed_output = jnp.stack(outputs).reshape(tokens_here, heads_here * P_SIZE)
    gated = mixed_output * jax.nn.silu(gate_input.astype(jnp.float32))
    squares = lax.psum(jnp.sum(gated * gated, axis=1), "head")
    scale = lax.rsqrt(squares / (MIXER_HEADS * P_SIZE) + 1e-05)
    return (gated * scale[:, None] * norm_gain).astype(jnp.bfloat16)


def attention(queries, keys, values):
    tokens_here = queries.shape[0]
    kv_here = keys.shape[1] // DH
    per_kv = HQ // KVH
    query_rows = queries.reshape(tokens_here, kv_here, per_kv, DH)
    first = lax.axis_index("ctx") * tokens_here
    query_pos = first + jnp.arange(tokens_here, dtype=jnp.int32)
    factor = DH ** (-0.5)

    def update(carry, key_block, value_block, key_pos):
        peak, total_sum, summed = carry
        score = (
            jnp.einsum("tgqd,jgd->gqtj", query_rows, key_block, preferred_element_type=jnp.float32)
            * factor
        )
        mask = (key_pos[None, :] <= query_pos[:, None])[None, None]
        block_peak = jnp.max(jnp.where(mask, score, -1e30), axis=-1)
        new_peak = jnp.maximum(peak, block_peak)
        weight = jnp.where(mask, jnp.exp(score - new_peak[..., None]), 0.0)
        shrink = jnp.exp(peak - new_peak)
        total_sum = total_sum * shrink + jnp.sum(weight, axis=-1)
        summed = summed * shrink[..., None] + jnp.einsum(
            "gqtj,jgd->gqtd",
            weight.astype(jnp.bfloat16),
            value_block,
            preferred_element_type=jnp.float32,
        )
        return (new_peak, total_sum, summed)

    initial = (
        jnp.full((kv_here, per_kv, tokens_here), -1e30, jnp.float32),
        jnp.zeros((kv_here, per_kv, tokens_here), jnp.float32),
        jnp.zeros((kv_here, per_kv, tokens_here, DH), jnp.float32),
    )
    carry = initial
    key_piece = lax.all_gather(keys, "ctx", axis=0, tiled=True)
    value_piece = lax.all_gather(values, "ctx", axis=0, tiled=True)
    rows = key_piece.shape[0]
    width = 512
    number = rows // width
    key_blocks = key_piece.reshape(number, width, kv_here, DH)
    value_blocks = value_piece.reshape(number, width, kv_here, DH)

    def advance(inner, block_slice):
        key_block, value_block, index = block_slice
        block_start = index * width
        key_pos = block_start + jnp.arange(width, dtype=jnp.int32)
        inner = update(inner, key_block, value_block, key_pos)
        return (inner, None)

    carry, _ = lax.scan(
        advance, carry, (key_blocks, value_blocks, jnp.arange(number, dtype=jnp.int32))
    )
    peak, total_sum, summed = carry
    result = summed / total_sum[..., None]
    result = jnp.transpose(result, (2, 0, 1, 3)).reshape(tokens_here, kv_here * per_kv * DH)
    return result.astype(jnp.bfloat16)


def per_device(
    ssm_input,
    gate_input,
    in_state,
    out_state,
    step_size,
    log_decay,
    skip_gain,
    norm_gain,
    queries,
    keys,
    values,
):
    mamba_out = mamba_mixer(
        ssm_input, gate_input, in_state, out_state, step_size, log_decay, skip_gain, norm_gain
    )
    attention_out = attention(queries, keys, values)
    return (mamba_out, attention_out)


def solution(mesh):
    return jax.shard_map(
        per_device,
        mesh=mesh,
        in_specs=(
            P("ctx", "head"),
            P("ctx", "head"),
            P("ctx", "head"),
            P("ctx", "head"),
            P("ctx", "head"),
            P("ctx", "head"),
            P("head"),
            P("head"),
            P("ctx", "head"),
            P("ctx", "head"),
            P("ctx", "head"),
        ),
        out_specs=(P("ctx", "head"), P("ctx", "head")),
        check_vma=False,
    )
```

profile of v0, /device:TPU:231, one launch (start us, length us, event | category | flops | bytes accessed | tf_op | source)
XLA Modules:
  0.0 396.7 jit_solution(6865414195518606855)
XLA Ops:
  15.9 28.9 %all_gather.16 = bf16[32,1,16]{2,1,0:T(2,128)(2,1)S(1)} all-gather(bf16[1,1,16]{2,1,0:T(2,128)(2,1)S(1)} %get-tuple-element.226), channel_id=1, replica_groups=mesh['ctx'=32,'head'=8] {'ctx'}, dimensions={0}, use_global_device_ids=true | all-gather | bytes 1056 | tf_op jit(solution)/shard_map/all_gather | solution.py:19
  46.8 6.7 %fusion.40 = f32[256,1,16,64]{0,3,2,1:T(8,128)} fusion(f32[256,256]{1,0:T(8,128)S(1)} %copy.73, f32[256,16]{0,1:T(8,128)S(1)} %copy.71, pred[256,256]{1,0:T(8,128)(4,1)} %iota_compare_fusion, f32[256,16,64]{0,2,1:T(8,128)S(1)} %bitcast.182, f32[256,16]{0,1:T(8,128)S(1)} %copy-done.3), kind=kOutput, calls=%fused_computation.47 | convolution fusion | flops 810811392 | bytes 2457600 | tf_op jit(solution)/shard_map/tsgk,sgkp->tgkp/dot_general | solution.py:47
  53.5 28.7 %all-gather.5.cloned.1.call-done = bf16[8192,128]{1,0:T(8,128)(2,1)} async-done(((bf16[256,128]{1,0:T(8,128)(2,1)}), bf16[8192,128]{1,0:T(8,128)(2,1)}) %all-gather.5.cloned.1.call-update) | async-done | bytes 2097168 | tf_op jit(solution)/shard_map/all_gather | solution.py:139
  82.3 77.7 %all-gather.7.cloned.1.call-done = bf16[8192,128]{1,0:T(8,128)(2,1)} async-done(((bf16[256,128]{1,0:T(8,128)(2,1)}), bf16[8192,128]{1,0:T(8,128)(2,1)}) %all-gather.7.cloned.1.call-update) | async-done | bytes 2097168 | tf_op jit(solution)/shard_map/all_gather | solution.py:140
  160.0 157.5 %while.28 = (s32[]{:T(128)}, f32[1,8,256]{2,1,0:T(8,128)S(1)}, f32[1,8,256]{2,1,0:T(8,128)S(1)}, f32[1,8,256,128]{3,2,1,0:T(8,128)S(1)}, s32[16]{0:T(128)S(1)}, ...) while((s32[]{:T(128)}, f32[1,8,256]{2,1,0:T(8,128)S(1)}, ...), condition=%wide.region_9.10_spmd.clone, body=%wide.region_6.9_spmd.clone.sunk | while | flops 549335808 | bytes 32906428 | solution.py:154
  161.4 3.7 fusion.72
  165.1 3.8 fusion.75
  171.2 3.7 fusion.72
  174.9 3.8 fusion.75
  184.7 3.8 fusion.75
  190.9 3.7 fusion.72
  194.6 3.8 fusion.75
  200.8 3.7 fusion.72
  204.4 3.8 fusion.75
  210.6 3.7 fusion.72
  214.3 3.8 fusion.75
  224.1 3.9 fusion.75
  234.0 3.9 fusion.75
  243.9 3.8 fusion.75
  253.8 3.8 fusion.75
  260.0 3.7 fusion.72
  263.6 3.8 fusion.75
  273.5 3.8 fusion.75
  279.6 3.7 fusion.72
  283.3 3.8 fusion.75
  293.1 3.8 fusion.75
  299.3 3.7 fusion.72
  302.9 3.8 fusion.75
  309.1 3.7 fusion.72
  312.8 3.8 fusion.75
  319.2 48.5 %while.27 = (s32[]{:T(128)}, f32[1,16,128,64]{3,2,1,0:T(8,128)S(1)}, s32[]{:T(128)}, bf16[32,1,16]{2,1,0:T(2,128)(2,1)S(1)}, bf16[32,1,16,128,64]{3,4,2,0,1:T(8,128)(2,1)}, /*index=5*/s32[]{:T(128)}, s32[]{:T(128)}, s32[]{:T(128)}) while((s32[]{:T(128)}, f32[1,16,128,64]{3,2,1,0:T(8,128)S(1)}, s32[]{:T(128)}, ...), condition=%wide.region_3.4_spmd, body=%wide.region_2.3_spmd.sunk | while | flops 393237 | bytes 2359583 | solution.py:33
  371.8 16.2 %psum.7 = f32[256]{0:T(256)S(1)} all-reduce(f32[256]{0:T(256)S(1)} %multiply_reduce_fusion), channel_id=1, replica_groups=mesh['ctx'=32,'head'=8] {'head'}, use_global_device_ids=true, to_apply=%region_5.6 | all-reduce | flops 256 | bytes 2048 | tf_op jit(solution)/shard_map/psum | solution.py:99
  (345 shorter events, 117.7 us)
Async XLA Ops:
  7.2 37.7 %copy-start = (bf16[256,128]{1,0:T(8,128)(2,1)S(1)}, bf16[256,128]{1,0:T(8,128)(2,1)}, u32[]{:S(2)}) copy-start(bf16[256,128]{1,0:T(8,128)(2,1)} %param.18) | copy-start | bytes 196612
  7.2 37.7 %copy-start.2 = (bf16[256,128]{1,0:T(8,128)(2,1)S(1)}, bf16[256,128]{1,0:T(8,128)(2,1)}, u32[]{:S(2)}) copy-start(bf16[256,128]{1,0:T(8,128)(2,1)} %param.17) | copy-start | bytes 196612
  7.2 75.1 %all-gather.5.cloned.1.call-start = ((), (), s32[]{:S(2)}) async-start(), calls=%async_computation | async-start | bytes 2162688 | tf_op jit(solution)/shard_map/all_gather | solution.py:139
  7.9 152.1 %all-gather.7.cloned.1.call-start = ((), (), s32[]{:S(2)}) async-start(), calls=%async_computation.1 | async-start | bytes 2162688 | tf_op jit(solution)/shard_map/all_gather | solution.py:140
  8.7 310.4 %all-gather.9.cloned.1.call-start = ((), (), s32[]{:S(2)}) async-start(), calls=%async_computation.2 | async-start | bytes 8650752 | tf_op jit(solution)/shard_map/all_gather | solution.py:19
  12.1 34.8 %copy-start.3 = (f32[256,16]{0,1:T(8,128)S(1)}, f32[256,16]{0,1:T(8,128)}, u32[]{:S(2)}) copy-start(f32[256,16]{0,1:T(8,128)} %param.19) | copy-start | bytes 49156
  165.1 3.8 copy-start.1
  174.9 3.8 copy-start.1
  184.7 3.8 copy-start.1
  194.6 3.8 copy-start.1
  204.4 3.8 copy-start.1
  214.2 3.8 copy-start.1
  224.1 3.9 copy-start.1
  234.0 4.0 copy-start.1
  243.9 3.8 copy-start.1
  253.8 3.9 copy-start.1
  263.6 3.8 copy-start.1
  273.5 3.8 copy-start.1
  283.3 3.8 copy-start.1
  293.1 3.8 copy-start.1
  302.9 3.8 copy-start.1
  312.7 3.8 copy-start.1
  319.2 48.5 %copy-start.5 = (f32[16]{0:T(128)S(1)}, f32[16]{0:T(128)}, u32[]{:S(2)}) copy-start(f32[16]{0:T(128)} %param.21) | copy-start | bytes 196
  367.7 20.3 %copy-start.4 = (f32[1024]{0:T(1024)S(1)}, f32[1024]{0:T(1024)}, u32[]{:S(2)}) copy-start(f32[1024]{0:T(1024)} %param.22) | copy-start | bytes 12292
Sparse Core Ops, SparseCore 0:
  10.6 71.6 all-gather.4
  84.9 75.1 all-gather.6
  163.2 97.9 all-gather.8
where the time goes:
time: 399 us; the launch traced here: 397 us
  matrix products  131 us (33%)
  waiting for transfers between devices  108 us (27%)
  local copies, waits for them, and re-layouts  54.3 us (14%)
  blocking collectives  45.1 us (11%)
  other arithmetic  31.6 us (8%)
  between operations  13.9 us (3%)
  loops' own time  12.9 us (3%)
    all_gather x1, waiting for transfers between devices, attention(): value_piece = lax.all_gather(values, 'ctx', axis=0, tiled=True)  77.7 us
    dot_general x16, matrix products, update(): jnp.einsum('gqtj,jgd->gqtd', weight.astype(jnp.bfloat16), value_block, pr...  61 us
    dot_general x16, matrix products, update(): jnp.einsum('tgqd,jgd->gqtj', query_rows, key_block, preferred_element_typ...  58.5 us
    dynamic_slice x62, local copies, waits for them, and re-layouts, one(): lax.dynamic_index_in_dim(a, turn, 0, False).astype(own.dtype)  39 us
    all_gather x1, blocking collectives, carried_in(): lax.all_gather(a.astype(kind), axis)  28.9 us
    all_gather x1, waiting for transfers between devices, attention(): key_piece = lax.all_gather(keys, 'ctx', axis=0, tiled=True)  28.7 us
    psum x1, blocking collectives, mamba_mixer(): squares = lax.psum(jnp.sum(gated * gated, axis=1), 'head')  16.2 us
    reduce_sum x16, other arithmetic, update(): total_sum = total_sum * shrink + jnp.sum(weight, axis=-1)  14.1 us
  transfers between devices with their start and end apart: 3, of which 2 were waited for; matrix products, arithmetic and copies ran while one was open for 41% of the time, Pallas kernels for 0%

commit v1 on v0

--- a/solution.py
+++ b/solution.py
@@ -136,8 +136,11 @@
         jnp.zeros((kv_here, per_kv, tokens_here, DH), jnp.float32),
     )
     carry = initial
-    key_piece = lax.all_gather(keys, "ctx", axis=0, tiled=True)
-    value_piece = lax.all_gather(values, "ctx", axis=0, tiled=True)
+    key_piece, value_piece = jnp.split(
+        lax.all_gather(jnp.concatenate([keys, values], axis=1), "ctx", axis=0, tiled=True),
+        [keys.shape[1]],
+        axis=1,
+    )
     rows = key_piece.shape[0]
     width = 512
     number = rows // width

time: 399 us -> 330 us (0.83)
  waiting for transfers between devices: 108 us -> 35 us
  local copies, waits for them, and re-layouts: 54.3 us -> 58.7 us
    all_gather x2 -> x1, waiting for transfers between devices: 106 us -> 34.9 us  [attention(): lax.all_gather(jnp.concatenate([keys, values], axis=1), 'ctx', axis=0, ti...]
    split x0 -> x1, local copies, waits for them, and re-layouts: none -> 4.45 us  [attention(): jnp.split(lax.all_gather(jnp.concatenate([keys, values], axis=1), 'ctx',...]
  transfers between devices with their start and end apart: 3 -> 2, of which waited for: 2 -> 1; matrix products, arithmetic and copies ran while one was open for 41% -> 51% of each run, Pallas kernels for 0% -> 0%
where the time goes in v1:
time: 330 us; the launch traced here: 328 us
  matrix products  130 us (39%)
  local copies, waits for them, and re-layouts  58.7 us (18%)
  blocking collectives  44.5 us (13%)
  waiting for transfers between devices  35 us (11%)
  other arithmetic  32.9 us (10%)
  between operations  14.2 us (4%)
  loops' own time  13 us (4%)
    dot_general x16, matrix products, update(): jnp.einsum('gqtj,jgd->gqtd', weight.astype(jnp.bfloat16), value_block, pr...  60.9 us
    dot_general x16, matrix products, update(): jnp.einsum('tgqd,jgd->gqtj', query_rows, key_block, preferred_element_typ...  58.6 us
    dynamic_slice x62, local copies, waits for them, and re-layouts, one(): lax.dynamic_index_in_dim(a, turn, 0, False).astype(own.dtype)  39 us
    all_gather x1, waiting for transfers between devices, attention(): lax.all_gather(jnp.concatenate([keys, values], axis=1), 'ctx', axis=0, ti...  34.9 us
    all_gather x1, blocking collectives, carried_in(): lax.all_gather(a.astype(kind), axis)  28.4 us
    psum x1, blocking collectives, mamba_mixer(): squares = lax.psum(jnp.sum(gated * gated, axis=1), 'head')  16 us
    reduce_sum x16, other arithmetic, update(): total_sum = total_sum * shrink + jnp.sum(weight, axis=-1)  13.9 us
    another operation x1, loops' own time, attention(): lax.scan(advance, carry, (key_blocks, value_blocks, jnp.arange(number, dt...  11.6 us
  transfers between devices with their start and end apart: 2, of which 1 were waited for; matrix products, arithmetic and copies ran while one was open for 51% of the time, Pallas kernels for 0%

profile of v1, /device:TPU:231, one launch (start us, length us, event | category | flops | bytes accessed | tf_op | source)
XLA Modules:
  0.0 328.3 jit_solution(8471002405693364448)
XLA Ops:
  15.2 28.4 %all_gather.13 = bf16[32,1,16]{2,1,0:T(2,128)(2,1)S(1)} all-gather(bf16[1,1,16]{2,1,0:T(2,128)(2,1)S(1)} %get-tuple-element.228), channel_id=1, replica_groups=mesh['ctx'=32,'head'=8] {'ctx'}, dimensions={0}, use_global_device_ids=true | all-gather | bytes 1056 | tf_op jit(solution)/shard_map/all_gather | solution.py:19
  45.7 6.7 %fusion.40 = f32[256,1,16,64]{0,3,2,1:T(8,128)} fusion(f32[256,256]{1,0:T(8,128)S(1)} %copy.73, f32[256,16]{0,1:T(8,128)S(1)} %copy.71, pred[256,256]{1,0:T(8,128)(4,1)} %iota_compare_fusion, f32[256,16,64]{0,2,1:T(8,128)S(1)} %bitcast.182, f32[256,16]{0,1:T(8,128)S(1)} %copy-done.3), kind=kOutput, calls=%fused_computation.47 | convolution fusion | flops 810811392 | bytes 2457600 | tf_op jit(solution)/shard_map/tsgk,sgkp->tgkp/dot_general | solution.py:47
  52.4 34.9 %all-gather.4.cloned.1.call-done = bf16[8192,256]{1,0:T(8,128)(2,1)} async-done(((bf16[256,256]{1,0:T(8,128)(2,1)}), bf16[8192,256]{1,0:T(8,128)(2,1)}) %all-gather.4.cloned.1.call-update) | async-done | bytes 4194320 | tf_op jit(solution)/shard_map/all_gather | solution.py:140
  87.3 4.5 %fusion.60 = (bf16[8192,128]{1,0:T(8,128)(2,1)}, bf16[8192,128]{1,0:T(8,128)(2,1)}) fusion(bf16[8192,256]{1,0:T(8,128)(2,1)} %all-gather.4.cloned.1.call-done), kind=kLoop, calls=%fused_computation.87 | loop fusion | bytes 8388608 | tf_op jit(solution)/shard_map/split | solution.py:139
  91.8 157.2 %while.28 = (s32[]{:T(128)}, f32[1,8,256]{2,1,0:T(8,128)S(1)}, f32[1,8,256]{2,1,0:T(8,128)S(1)}, f32[1,8,256,128]{3,2,1,0:T(8,128)S(1)}, s32[16]{0:T(128)S(1)}, ...) while((s32[]{:T(128)}, f32[1,8,256]{2,1,0:T(8,128)S(1)}, ...), condition=%wide.region_9.10_spmd.clone, body=%wide.region_6.9_spmd.clone.sunk | while | flops 549335808 | bytes 32906428 | solution.py:157
  96.8 3.8 %fusion.76 = f32[1,8,256,128]{3,2,1,0:T(8,128)S(1)} fusion(f32[512,256,8]{1,0,2:T(8,128)} %get-tuple-element.322, f32[8,256]{1,0:T(8,128)S(1)} %bitcast.187, pred[256,512]{0,1:T(8,128)(4,1)S(1)} %broadcast_compare_fusion.2, f32[1,8,256,128]{3,2,1,0:T(8,128)S(1)} %get-tuple-element.363, f32[8,256]{1,0:T(8,128)S(1)} %get-tuple-element.323, ...), kind=kOutput, calls=%fused_computation.15.clone.1 | convolution fusion | flops 273416192 | bytes 6570497 | tf_op jit(solution)/shard_map/while/body/eval_jaxpr/gqtj,jgd->gqtd/dot_general | solution.py:125
  106.6 3.9 %fusion.76 = f32[1,8,256,128]{3,2,1,0:T(8,128)S(1)} fusion(f32[512,256,8]{1,0,2:T(8,128)} %get-tuple-element.322, f32[8,256]{1,0:T(8,128)S(1)} %bitcast.187, pred[256,512]{0,1:T(8,128)(4,1)S(1)} %broadcast_compare_fusion.2, f32[1,8,256,128]{3,2,1,0:T(8,128)S(1)} %get-tuple-element.363, f32[8,256]{1,0:T(8,128)S(1)} %get-tuple-element.323, ...), kind=kOutput, calls=%fused_computation.15.clone.1 | convolution fusion | flops 273416192 | bytes 6570497 | tf_op jit(solution)/shard_map/while/body/eval_jaxpr/gqtj,jgd->gqtd/dot_general | solution.py:125
  112.9 3.7 %fusion.73 = (f32[8,256]{1,0:T(8,128)S(1)}, f32[512,256,8]{1,0,2:T(8,128)}) fusion(pred[256,512]{0,1:T(8,128)(4,1)S(1)} %broadcast_compare_fusion.2, bf16[256,1,8,128]{3,0,2,1:T(8,128)(2,1)S(1)} %get-tuple-element.378, bf16[16,512,1,128]{3,1,2,0:T(8,128)(2,1)} %get-tuple-element.377, s32[]{:T(128)} %get-tuple-element.360), kind=kOutput, calls=%fused_computation.6.clone.1 | convolution fusion | flops 271579136 | bytes 4989440 | tf_op jit(solution)/shard_map/while/body/eval_jaxpr/tgqd,jgd->gqtj/dot_general | solution.py:116
  116.5 3.8 %fusion.76 = f32[1,8,256,128]{3,2,1,0:T(8,128)S(1)} fusion(f32[512,256,8]{1,0,2:T(8,128)} %get-tuple-element.322, f32[8,256]{1,0:T(8,128)S(1)} %bitcast.187, pred[256,512]{0,1:T(8,128)(4,1)S(1)} %broadcast_compare_fusion.2, f32[1,8,256,128]{3,2,1,0:T(8,128)S(1)} %get-tuple-element.363, f32[8,256]{1,0:T(8,128)S(1)} %get-tuple-element.323, ...), kind=kOutput, calls=%fused_computation.15.clone.1 | convolution fusion | flops 273416192 | bytes 6570497 | tf_op jit(solution)/shard_map/while/body/eval_jaxpr/gqtj,jgd->gqtd/dot_general | solution.py:125
  126.4 3.8 %fusion.76 = f32[1,8,256,128]{3,2,1,0:T(8,128)S(1)} fusion(f32[512,256,8]{1,0,2:T(8,128)} %get-tuple-element.322, f32[8,256]{1,0:T(8,128)S(1)} %bitcast.187, pred[256,512]{0,1:T(8,128)(4,1)S(1)} %broadcast_compare_fusion.2, f32[1,8,256,128]{3,2,1,0:T(8,128)S(1)} %get-tuple-element.363, f32[8,256]{1,0:T(8,128)S(1)} %get-tuple-element.323, ...), kind=kOutput, calls=%fused_computation.15.clone.1 | convolution fusion | flops 273416192 | bytes 6570497 | tf_op jit(solution)/shard_map/while/body/eval_jaxpr/gqtj,jgd->gqtd/dot_general | solution.py:125
  136.2 3.8 %fusion.76 = f32[1,8,256,128]{3,2,1,0:T(8,128)S(1)} fusion(f32[512,256,8]{1,0,2:T(8,128)} %get-tuple-element.322, f32[8,256]{1,0:T(8,128)S(1)} %bitcast.187, pred[256,512]{0,1:T(8,128)(4,1)S(1)} %broadcast_compare_fusion.2, f32[1,8,256,128]{3,2,1,0:T(8,128)S(1)} %get-tuple-element.363, f32[8,256]{1,0:T(8,128)S(1)} %get-tuple-element.323, ...), kind=kOutput, calls=%fused_computation.15.clone.1 | convolution fusion | flops 273416192 | bytes 6570497 | tf_op jit(solution)/shard_map/while/body/eval_jaxpr/gqtj,jgd->gqtd/dot_general | solution.py:125
  146.0 3.8 %fusion.76 = f32[1,8,256,128]{3,2,1,0:T(8,128)S(1)} fusion(f32[512,256,8]{1,0,2:T(8,128)} %get-tuple-element.322, f32[8,256]{1,0:T(8,128)S(1)} %bitcast.187, pred[256,512]{0,1:T(8,128)(4,1)S(1)} %broadcast_compare_fusion.2, f32[1,8,256,128]{3,2,1,0:T(8,128)S(1)} %get-tuple-element.363, f32[8,256]{1,0:T(8,128)S(1)} %get-tuple-element.323, ...), kind=kOutput, calls=%fused_computation.15.clone.1 | convolution fusion | flops 273416192 | bytes 6570497 | tf_op jit(solution)/shard_map/while/body/eval_jaxpr/gqtj,jgd->gqtd/dot_general | solution.py:125
  152.1 3.7 %fusion.73 = (f32[8,256]{1,0:T(8,128)S(1)}, f32[512,256,8]{1,0,2:T(8,128)}) fusion(pred[256,512]{0,1:T(8,128)(4,1)S(1)} %broadcast_compare_fusion.2, bf16[256,1,8,128]{3,0,2,1:T(8,128)(2,1)S(1)} %get-tuple-element.378, bf16[16,512,1,128]{3,1,2,0:T(8,128)(2,1)} %get-tuple-element.377, s32[]{:T(128)} %get-tuple-element.360), kind=kOutput, calls=%fused_computation.6.clone.1 | convolution fusion | flops 271579136 | bytes 4989440 | tf_op jit(solution)/shard_map/while/body/eval_jaxpr/tgqd,jgd->gqtj/dot_general | solution.py:116
  155.8 3.8 %fusion.76 = f32[1,8,256,128]{3,2,1,0:T(8,128)S(1)} fusion(f32[512,256,8]{1,0,2:T(8,128)} %get-tuple-element.322, f32[8,256]{1,0:T(8,128)S(1)} %bitcast.187, pred[256,512]{0,1:T(8,128)(4,1)S(1)} %broadcast_compare_fusion.2, f32[1,8,256,128]{3,2,1,0:T(8,128)S(1)} %get-tuple-element.363, f32[8,256]{1,0:T(8,128)S(1)} %get-tuple-element.323, ...), kind=kOutput, calls=%fused_computation.15.clone.1 | convolution fusion | flops 273416192 | bytes 6570497 | tf_op jit(solution)/shard_map/while/body/eval_jaxpr/gqtj,jgd->gqtd/dot_general | solution.py:125
  165.6 3.9 %fusion.76 = f32[1,8,256,128]{3,2,1,0:T(8,128)S(1)} fusion(f32[512,256,8]{1,0,2:T(8,128)} %get-tuple-element.322, f32[8,256]{1,0:T(8,128)S(1)} %bitcast.187, pred[256,512]{0,1:T(8,128)(4,1)S(1)} %broadcast_compare_fusion.2, f32[1,8,256,128]{3,2,1,0:T(8,128)S(1)} %get-tuple-element.363, f32[8,256]{1,0:T(8,128)S(1)} %get-tuple-element.323, ...), kind=kOutput, calls=%fused_computation.15.clone.1 | convolution fusion | flops 273416192 | bytes 6570497 | tf_op jit(solution)/shard_map/while/body/eval_jaxpr/gqtj,jgd->gqtd/dot_general | solution.py:125
  175.5 3.8 %fusion.76 = f32[1,8,256,128]{3,2,1,0:T(8,128)S(1)} fusion(f32[512,256,8]{1,0,2:T(8,128)} %get-tuple-element.322, f32[8,256]{1,0:T(8,128)S(1)} %bitcast.187, pred[256,512]{0,1:T(8,128)(4,1)S(1)} %broadcast_compare_fusion.2, f32[1,8,256,128]{3,2,1,0:T(8,128)S(1)} %get-tuple-element.363, f32[8,256]{1,0:T(8,128)S(1)} %get-tuple-element.323, ...), kind=kOutput, calls=%fused_computation.15.clone.1 | convolution fusion | flops 273416192 | bytes 6570497 | tf_op jit(solution)/shard_map/while/body/eval_jaxpr/gqtj,jgd->gqtd/dot_general | solution.py:125
  181.7 3.7 %fusion.73 = (f32[8,256]{1,0:T(8,128)S(1)}, f32[512,256,8]{1,0,2:T(8,128)}) fusion(pred[256,512]{0,1:T(8,128)(4,1)S(1)} %broadcast_compare_fusion.2, bf16[256,1,8,128]{3,0,2,1:T(8,128)(2,1)S(1)} %get-tuple-element.378, bf16[16,512,1,128]{3,1,2,0:T(8,128)(2,1)} %get-tuple-element.377, s32[]{:T(128)} %get-tuple-element.360), kind=kOutput, calls=%fused_computation.6.clone.1 | convolution fusion | flops 271579136 | bytes 4989440 | tf_op jit(solution)/shard_map/while/body/eval_jaxpr/tgqd,jgd->gqtj/dot_general | solution.py:116
  185.3 3.8 %fusion.76 = f32[1,8,256,128]{3,2,1,0:T(8,128)S(1)} fusion(f32[512,256,8]{1,0,2:T(8,128)} %get-tuple-element.322, f32[8,256]{1,0:T(8,128)S(1)} %bitcast.187, pred[256,512]{0,1:T(8,128)(4,1)S(1)} %broadcast_compare_fusion.2, f32[1,8,256,128]{3,2,1,0:T(8,128)S(1)} %get-tuple-element.363, f32[8,256]{1,0:T(8,128)S(1)} %get-tuple-element.323, ...), kind=kOutput, calls=%fused_computation.15.clone.1 | convolution fusion | flops 273416192 | bytes 6570497 | tf_op jit(solution)/shard_map/while/body/eval_jaxpr/gqtj,jgd->gqtd/dot_general | solution.py:125
  191.5 3.7 %fusion.73 = (f32[8,256]{1,0:T(8,128)S(1)}, f32[512,256,8]{1,0,2:T(8,128)}) fusion(pred[256,512]{0,1:T(8,128)(4,1)S(1)} %broadcast_compare_fusion.2, bf16[256,1,8,128]{3,0,2,1:T(8,128)(2,1)S(1)} %get-tuple-element.378, bf16[16,512,1,128]{3,1,2,0:T(8,128)(2,1)} %get-tuple-element.377, s32[]{:T(128)} %get-tuple-element.360), kind=kOutput, calls=%fused_computation.6.clone.1 | convolution fusion | flops 271579136 | bytes 4989440 | tf_op jit(solution)/shard_map/while/body/eval_jaxpr/tgqd,jgd->gqtj/dot_general | solution.py:116
  195.2 3.8 %fusion.76 = f32[1,8,256,128]{3,2,1,0:T(8,128)S(1)} fusion(f32[512,256,8]{1,0,2:T(8,128)} %get-tuple-element.322, f32[8,256]{1,0:T(8,128)S(1)} %bitcast.187, pred[256,512]{0,1:T(8,128)(4,1)S(1)} %broadcast_compare_fusion.2, f32[1,8,256,128]{3,2,1,0:T(8,128)S(1)} %get-tuple-element.363, f32[8,256]{1,0:T(8,128)S(1)} %get-tuple-element.323, ...), kind=kOutput, calls=%fused_computation.15.clone.1 | convolution fusion | flops 273416192 | bytes 6570497 | tf_op jit(solution)/shard_map/while/body/eval_jaxpr/gqtj,jgd->gqtd/dot_general | solution.py:125
  201.3 3.7 %fusion.73 = (f32[8,256]{1,0:T(8,128)S(1)}, f32[512,256,8]{1,0,2:T(8,128)}) fusion(pred[256,512]{0,1:T(8,128)(4,1)S(1)} %broadcast_compare_fusion.2, bf16[256,1,8,128]{3,0,2,1:T(8,128)(2,1)S(1)} %get-tuple-element.378, bf16[16,512,1,128]{3,1,2,0:T(8,128)(2,1)} %get-tuple-element.377, s32[]{:T(128)} %get-tuple-element.360), kind=kOutput, calls=%fused_computation.6.clone.1 | convolution fusion | flops 271579136 | bytes 4989440 | tf_op jit(solution)/shard_map/while/body/eval_jaxpr/tgqd,jgd->gqtj/dot_general | solution.py:116
  205.0 3.8 %fusion.76 = f32[1,8,256,128]{3,2,1,0:T(8,128)S(1)} fusion(f32[512,256,8]{1,0,2:T(8,128)} %get-tuple-element.322, f32[8,256]{1,0:T(8,128)S(1)} %bitcast.187, pred[256,512]{0,1:T(8,128)(4,1)S(1)} %broadcast_compare_fusion.2, f32[1,8,256,128]{3,2,1,0:T(8,128)S(1)} %get-tuple-element.363, f32[8,256]{1,0:T(8,128)S(1)} %get-tuple-element.323, ...), kind=kOutput, calls=%fused_computation.15.clone.1 | convolution fusion | flops 273416192 | bytes 6570497 | tf_op jit(solution)/shard_map/while/body/eval_jaxpr/gqtj,jgd->gqtd/dot_general | solution.py:125
  211.1 3.7 %fusion.73 = (f32[8,256]{1,0:T(8,128)S(1)}, f32[512,256,8]{1,0,2:T(8,128)}) fusion(pred[256,512]{0,1:T(8,128)(4,1)S(1)} %broadcast_compare_fusion.2, bf16[256,1,8,128]{3,0,2,1:T(8,128)(2,1)S(1)} %get-tuple-element.378, bf16[16,512,1,128]{3,1,2,0:T(8,128)(2,1)} %get-tuple-element.377, s32[]{:T(128)} %get-tuple-element.360), kind=kOutput, calls=%fused_computation.6.clone.1 | convolution fusion | flops 271579136 | bytes 4989440 | tf_op jit(solution)/shard_map/while/body/eval_jaxpr/tgqd,jgd->gqtj/dot_general | solution.py:116
  214.8 3.8 %fusion.76 = f32[1,8,256,128]{3,2,1,0:T(8,128)S(1)} fusion(f32[512,256,8]{1,0,2:T(8,128)} %get-tuple-element.322, f32[8,256]{1,0:T(8,128)S(1)} %bitcast.187, pred[256,512]{0,1:T(8,128)(4,1)S(1)} %broadcast_compare_fusion.2, f32[1,8,256,128]{3,2,1,0:T(8,128)S(1)} %get-tuple-element.363, f32[8,256]{1,0:T(8,128)S(1)} %get-tuple-element.323, ...), kind=kOutput, calls=%fused_computation.15.clone.1 | convolution fusion | flops 273416192 | bytes 6570497 | tf_op jit(solution)/shard_map/while/body/eval_jaxpr/gqtj,jgd->gqtd/dot_general | solution.py:125
  220.9 3.7 %fusion.73 = (f32[8,256]{1,0:T(8,128)S(1)}, f32[512,256,8]{1,0,2:T(8,128)}) fusion(pred[256,512]{0,1:T(8,128)(4,1)S(1)} %broadcast_compare_fusion.2, bf16[256,1,8,128]{3,0,2,1:T(8,128)(2,1)S(1)} %get-tuple-element.378, bf16[16,512,1,128]{3,1,2,0:T(8,128)(2,1)} %get-tuple-element.377, s32[]{:T(128)} %get-tuple-element.360), kind=kOutput, calls=%fused_computation.6.clone.1 | convolution fusion | flops 271579136 | bytes 4989440 | tf_op jit(solution)/shard_map/while/body/eval_jaxpr/tgqd,jgd->gqtj/dot_general | solution.py:116
  224.6 3.8 %fusion.76 = f32[1,8,256,128]{3,2,1,0:T(8,128)S(1)} fusion(f32[512,256,8]{1,0,2:T(8,128)} %get-tuple-element.322, f32[8,256]{1,0:T(8,128)S(1)} %bitcast.187, pred[256,512]{0,1:T(8,128)(4,1)S(1)} %broadcast_compare_fusion.2, f32[1,8,256,128]{3,2,1,0:T(8,128)S(1)} %get-tuple-element.363, f32[8,256]{1,0:T(8,128)S(1)} %get-tuple-element.323, ...), kind=kOutput, calls=%fused_computation.15.clone.1 | convolution fusion | flops 273416192 | bytes 6570497 | tf_op jit(solution)/shard_map/while/body/eval_jaxpr/gqtj,jgd->gqtd/dot_general | solution.py:125
  230.7 3.7 %fusion.73 = (f32[8,256]{1,0:T(8,128)S(1)}, f32[512,256,8]{1,0,2:T(8,128)}) fusion(pred[256,512]{0,1:T(8,128)(4,1)S(1)} %broadcast_compare_fusion.2, bf16[256,1,8,128]{3,0,2,1:T(8,128)(2,1)S(1)} %get-tuple-element.378, bf16[16,512,1,128]{3,1,2,0:T(8,128)(2,1)} %get-tuple-element.377, s32[]{:T(128)} %get-tuple-element.360), kind=kOutput, calls=%fused_computation.6.clone.1 | convolution fusion | flops 271579136 | bytes 4989440 | tf_op jit(solution)/shard_map/while/body/eval_jaxpr/tgqd,jgd->gqtj/dot_general | solution.py:116
  234.4 3.8 %fusion.76 = f32[1,8,256,128]{3,2,1,0:T(8,128)S(1)} fusion(f32[512,256,8]{1,0,2:T(8,128)} %get-tuple-element.322, f32[8,256]{1,0:T(8,128)S(1)} %bitcast.187, pred[256,512]{0,1:T(8,128)(4,1)S(1)} %broadcast_compare_fusion.2, f32[1,8,256,128]{3,2,1,0:T(8,128)S(1)} %get-tuple-element.363, f32[8,256]{1,0:T(8,128)S(1)} %get-tuple-element.323, ...), kind=kOutput, calls=%fused_computation.15.clone.1 | convolution fusion | flops 273416192 | bytes 6570497 | tf_op jit(solution)/shard_map/while/body/eval_jaxpr/gqtj,jgd->gqtd/dot_general | solution.py:125
  240.5 3.7 %fusion.73 = (f32[8,256]{1,0:T(8,128)S(1)}, f32[512,256,8]{1,0,2:T(8,128)}) fusion(pred[256,512]{0,1:T(8,128)(4,1)S(1)} %broadcast_compare_fusion.2, bf16[256,1,8,128]{3,0,2,1:T(8,128)(2,1)S(1)} %get-tuple-element.378, bf16[16,512,1,128]{3,1,2,0:T(8,128)(2,1)} %get-tuple-element.377, s32[]{:T(128)} %get-tuple-element.360), kind=kOutput, calls=%fused_computation.6.clone.1 | convolution fusion | flops 271579136 | bytes 4989440 | tf_op jit(solution)/shard_map/while/body/eval_jaxpr/tgqd,jgd->gqtj/dot_general | solution.py:116
  244.2 3.8 %fusion.76 = f32[1,8,256,128]{3,2,1,0:T(8,128)S(1)} fusion(f32[512,256,8]{1,0,2:T(8,128)} %get-tuple-element.322, f32[8,256]{1,0:T(8,128)S(1)} %bitcast.187, pred[256,512]{0,1:T(8,128)(4,1)S(1)} %broadcast_compare_fusion.2, f32[1,8,256,128]{3,2,1,0:T(8,128)S(1)} %get-tuple-element.363, f32[8,256]{1,0:T(8,128)S(1)} %get-tuple-element.323, ...), kind=kOutput, calls=%fused_computation.15.clone.1 | convolution fusion | flops 273416192 | bytes 6570497 | tf_op jit(solution)/shard_map/while/body/eval_jaxpr/gqtj,jgd->gqtd/dot_general | solution.py:125
  250.6 48.5 %while.27 = (s32[]{:T(128)}, f32[1,16,128,64]{3,2,1,0:T(8,128)S(1)}, s32[]{:T(128)}, bf16[32,1,16]{2,1,0:T(2,128)(2,1)S(1)}, bf16[32,1,16,128,64]{3,4,2,0,1:T(8,128)(2,1)}, /*index=5*/s32[]{:T(128)}, s32[]{:T(128)}, s32[]{:T(128)}) while((s32[]{:T(128)}, f32[1,16,128,64]{3,2,1,0:T(8,128)S(1)}, s32[]{:T(128)}, ...), condition=%wide.region_3.4_spmd, body=%wide.region_2.3_spmd.sunk | while | flops 393237 | bytes 2359583 | solution.py:33
  303.3 16.0 %psum.7 = f32[256]{0:T(256)S(1)} all-reduce(f32[256]{0:T(256)S(1)} %multiply_reduce_fusion), channel_id=1, replica_groups=mesh['ctx'=32,'head'=8] {'head'}, use_global_device_ids=true, to_apply=%region_5.6 | all-reduce | flops 256 | bytes 2048 | tf_op jit(solution)/shard_map/psum | solution.py:99
  (344 shorter events, 116.7 us)
Async XLA Ops:
  7.2 36.6 %copy-start = (bf16[256,128]{1,0:T(8,128)(2,1)S(1)}, bf16[256,128]{1,0:T(8,128)(2,1)}, u32[]{:S(2)}) copy-start(bf16[256,128]{1,0:T(8,128)(2,1)} %param.18) | copy-start | bytes 196612
  7.2 6.0 %copy-start.2 = (bf16[256,128]{1,0:T(8,128)(2,1)S(1)}, bf16[256,128]{1,0:T(8,128)(2,1)}, u32[]{:S(2)}) copy-start(bf16[256,128]{1,0:T(8,128)(2,1)} %param.17) | copy-start | bytes 196612
  7.2 80.1 %all-gather.4.cloned.1.call-start = ((), (), s32[]{:S(2)}) async-start(), calls=%async_computation | async-start | bytes 4325376 | tf_op jit(solution)/shard_map/all_gather | solution.py:140
  8.8 241.7 %all-gather.6.cloned.1.call-start = ((), (), s32[]{:S(2)}) async-start(), calls=%async_computation.1 | async-start | bytes 8650752 | tf_op jit(solution)/shard_map/all_gather | solution.py:19
  12.2 33.4 %copy-start.3 = (f32[256,16]{0,1:T(8,128)S(1)}, f32[256,16]{0,1:T(8,128)}, u32[]{:S(2)}) copy-start(f32[256,16]{0,1:T(8,128)} %param.19) | copy-start | bytes 49156
  96.8 3.8 %copy-start.1 = (f32[512,256,8]{1,0,2:T(8,128)S(1)}, f32[512,256,8]{1,0,2:T(8,128)}, u32[]{:S(2)}) copy-start(f32[512,256,8]{1,0,2:T(8,128)} %get-tuple-element.322) | copy-start | bytes 12582916 | tf_op jit(solution)/shard_map/while
  106.6 3.9 %copy-start.1 = (f32[512,256,8]{1,0,2:T(8,128)S(1)}, f32[512,256,8]{1,0,2:T(8,128)}, u32[]{:S(2)}) copy-start(f32[512,256,8]{1,0,2:T(8,128)} %get-tuple-element.322) | copy-start | bytes 12582916 | tf_op jit(solution)/shard_map/while
  116.5 3.8 %copy-start.1 = (f32[512,256,8]{1,0,2:T(8,128)S(1)}, f32[512,256,8]{1,0,2:T(8,128)}, u32[]{:S(2)}) copy-start(f32[512,256,8]{1,0,2:T(8,128)} %get-tuple-element.322) | copy-start | bytes 12582916 | tf_op jit(solution)/shard_map/while
  126.3 3.8 %copy-start.1 = (f32[512,256,8]{1,0,2:T(8,128)S(1)}, f32[512,256,8]{1,0,2:T(8,128)}, u32[]{:S(2)}) copy-start(f32[512,256,8]{1,0,2:T(8,128)} %get-tuple-element.322) | copy-start | bytes 12582916 | tf_op jit(solution)/shard_map/while
  136.1 3.8 %copy-start.1 = (f32[512,256,8]{1,0,2:T(8,128)S(1)}, f32[512,256,8]{1,0,2:T(8,128)}, u32[]{:S(2)}) copy-start(f32[512,256,8]{1,0,2:T(8,128)} %get-tuple-element.322) | copy-start | bytes 12582916 | tf_op jit(solution)/shard_map/while
  146.0 3.8 %copy-start.1 = (f32[512,256,8]{1,0,2:T(8,128)S(1)}, f32[512,256,8]{1,0,2:T(8,128)}, u32[]{:S(2)}) copy-start(f32[512,256,8]{1,0,2:T(8,128)} %get-tuple-element.322) | copy-start | bytes 12582916 | tf_op jit(solution)/shard_map/while
  155.8 3.8 %copy-start.1 = (f32[512,256,8]{1,0,2:T(8,128)S(1)}, f32[512,256,8]{1,0,2:T(8,128)}, u32[]{:S(2)}) copy-start(f32[512,256,8]{1,0,2:T(8,128)} %get-tuple-element.322) | copy-start | bytes 12582916 | tf_op jit(solution)/shard_map/while
  165.6 3.9 %copy-start.1 = (f32[512,256,8]{1,0,2:T(8,128)S(1)}, f32[512,256,8]{1,0,2:T(8,128)}, u32[]{:S(2)}) copy-start(f32[512,256,8]{1,0,2:T(8,128)} %get-tuple-element.322) | copy-start | bytes 12582916 | tf_op jit(solution)/shard_map/while
  175.5 3.8 %copy-start.1 = (f32[512,256,8]{1,0,2:T(8,128)S(1)}, f32[512,256,8]{1,0,2:T(8,128)}, u32[]{:S(2)}) copy-start(f32[512,256,8]{1,0,2:T(8,128)} %get-tuple-element.322) | copy-start | bytes 12582916 | tf_op jit(solution)/shard_map/while
  185.3 3.8 %copy-start.1 = (f32[512,256,8]{1,0,2:T(8,128)S(1)}, f32[512,256,8]{1,0,2:T(8,128)}, u32[]{:S(2)}) copy-start(f32[512,256,8]{1,0,2:T(8,128)} %get-tuple-element.322) | copy-start | bytes 12582916 | tf_op jit(solution)/shard_map/while
  195.1 3.8 %copy-start.1 = (f32[512,256,8]{1,0,2:T(8,128)S(1)}, f32[512,256,8]{1,0,2:T(8,128)}, u32[]{:S(2)}) copy-start(f32[512,256,8]{1,0,2:T(8,128)} %get-tuple-element.322) | copy-start | bytes 12582916 | tf_op jit(solution)/shard_map/while
  205.0 3.8 %copy-start.1 = (f32[512,256,8]{1,0,2:T(8,128)S(1)}, f32[512,256,8]{1,0,2:T(8,128)}, u32[]{:S(2)}) copy-start(f32[512,256,8]{1,0,2:T(8,128)} %get-tuple-element.322) | copy-start | bytes 12582916 | tf_op jit(solution)/shard_map/while
  214.8 3.8 %copy-start.1 = (f32[512,256,8]{1,0,2:T(8,128)S(1)}, f32[512,256,8]{1,0,2:T(8,128)}, u32[]{:S(2)}) copy-start(f32[512,256,8]{1,0,2:T(8,128)} %get-tuple-element.322) | copy-start | bytes 12582916 | tf_op jit(solution)/shard_map/while
  224.6 3.8 %copy-start.1 = (f32[512,256,8]{1,0,2:T(8,128)S(1)}, f32[512,256,8]{1,0,2:T(8,128)}, u32[]{:S(2)}) copy-start(f32[512,256,8]{1,0,2:T(8,128)} %get-tuple-element.322) | copy-start | bytes 12582916 | tf_op jit(solution)/shard_map/while
  234.4 3.8 %copy-start.1 = (f32[512,256,8]{1,0,2:T(8,128)S(1)}, f32[512,256,8]{1,0,2:T(8,128)}, u32[]{:S(2)}) copy-start(f32[512,256,8]{1,0,2:T(8,128)} %get-tuple-element.322) | copy-start | bytes 12582916 | tf_op jit(solution)/shard_map/while
  244.2 3.8 %copy-start.1 = (f32[512,256,8]{1,0,2:T(8,128)S(1)}, f32[512,256,8]{1,0,2:T(8,128)}, u32[]{:S(2)}) copy-start(f32[512,256,8]{1,0,2:T(8,128)} %get-tuple-element.322) | copy-start | bytes 12582916 | tf_op jit(solution)/shard_map/while
  250.6 48.5 %copy-start.5 = (f32[16]{0:T(128)S(1)}, f32[16]{0:T(128)}, u32[]{:S(2)}) copy-start(f32[16]{0:T(128)} %param.21) | copy-start | bytes 196
  299.1 20.2 %copy-start.4 = (f32[1024]{0:T(1024)S(1)}, f32[1024]{0:T(1024)}, u32[]{:S(2)}) copy-start(f32[1024]{0:T(1024)} %param.22) | copy-start | bytes 12292
Sparse Core Ops, SparseCore 0:
  11.2 76.0 all-gather.3
  90.5 97.4 all-gather.5
